TPU v7x, 32 devices: a whole 2x2x4 slice. The times are simulated.
32 devices in a mesh: ens: 2 (over x), lon: 16 (over z, y, core).
Axes of the slice: x: 2, y: 2, z: 4, core: 2. Of those that a mesh axis runs over, the one named last changes fastest.
Arguments:
- tracer: float32 [4, 256, 75, 256], P(None, 'lon', None, 'ens'), parts along dimension 3, may hold values from -6 to 6
- east_speed: float32 [256, 75, 256], P('lon', None, 'ens'), parts along dimension 2, may hold values from -0.25 to 0.25
- north_speed: float32 [256, 75, 256], P('lon', None, 'ens'), parts along dimension 2, may hold values from -0.25 to 0.25
- diffusivity: float32 [256, 75, 256], P('lon', None, 'ens'), parts along dimension 2, may hold values from 0.02 to 0.2
- mixing: float32 [256, 75, 256], P('lon', None, 'ens'), parts along dimension 2, may hold values from 0.05 to 5
- thickness: float32 [256, 75, 256], P('lon', None, 'ens'), parts along dimension 2, may hold values from 0.5 to 2
- depth_levels: int32 [256, 256], P('lon', 'ens'), parts along dimension 1, may hold values from 0 to 75
- air_flux: float32 [8, 4096], P('ens', 'lon'), parts along dimension 0, may hold values from -6 to 6
- margin_tile: int32 [32768, 1], P(('ens', 'lon')), parts along dimension 0, may hold values from 0 to 15; in each aligned block of 1024 rows (0 to 1023, 1024 to 2047, ...) at most 64 rows name the same one
- margin_source: int32 [32768], P(('ens', 'lon')), parts along dimension 0, may hold values from 0 to 255
- margin_cell: int32 [32768], P(('ens', 'lon')), parts along dimension 0, may hold values from 0 to 2047
- margin_weight: float32 [32768], P(('ens', 'lon')), parts along dimension 0, may hold values from 0.2 to 1
Outputs:
- tracer_next: float32 [4, 256, 75, 256], P(None, 'lon', None, 'ens'), parts along dimension 3
There are 2 independent parts, one for each index of `ens`. A program takes and returns all parts, laid end to end along the dimension named above; each array names one. Nothing has to cross between parts.
Inputs may be any that keep to these rules, and one draw needn't show every extreme that they name: `margin_tile`: the rows of one tile name each ocean tile at most 64 times.
All inputs are finite; a program needn't handle non-finite values.
Results may differ from a plain program's by a relative error of at most 0.00002.
Values sent between devices are 32-bit elements; how exact they have to be, the bound alone decides.
No kernel may reach another device: no remote copies, remote signals or barrier semaphores. Data moves between devices by JAX's collectives and lax.ppermute only.
A program may use at most 192 MiB of HBM per device.

v0:
```python
import functools

import jax
import jax.numpy as jnp
from jax import lax
from jax.experimental import pallas as pl
from jax.experimental.pallas import tpu as pltpu
from jax.sharding import PartitionSpec as P

CAP = 64
HALF = 8
GROUP = 5
AHEAD = (2, 1, 0)
PACK_AHEAD = 2
LANES = 128
F32 = jnp.float32


def chunk_of(levels):
    return max(c for c in range(GROUP, 4 * GROUP, GROUP) if levels % c == 0)


def thirds(x):
    high = x.astype(jnp.bfloat16)
    rest = x - high.astype(F32)
    mid = rest.astype(jnp.bfloat16)
    low = (rest - mid.astype(F32)).astype(jnp.bfloat16)
    return high, mid, low


VMEM = pl.BlockSpec(memory_space=pltpu.VMEM)
ANY = pl.BlockSpec(memory_space=pl.ANY)


def in_hbm(*arrays):
    return [pltpu.with_memory_space_constraint(x, pltpu.HBM) for x in arrays]


def in_vmem(*arrays):
    return [pltpu.with_memory_space_constraint(x, pltpu.VMEM) for x in arrays]


def lane_ids(rows):
    return lax.broadcasted_iota(jnp.int32, (rows, LANES), 1)


def row_ids(rows):
    return lax.broadcasted_iota(jnp.int32, (rows, LANES), 0)


def dot_nt(a, b):
    return lax.dot_general(a, b, (((1,), (1,)), ((), ())), preferred_element_type=F32)


def sum_parts(stacked):
    rows = stacked.shape[0] // 3
    return stacked[:rows] + stacked[rows : 2 * rows] + stacked[2 * rows :]


def dot_nn(a, b):
    return lax.dot_general(a, b, (((1,), (0,)), ((), ())), preferred_element_type=F32)


def make_messages(tiles, air_ref, tile_ref, source_ref, cell_ref, weight_ref, msg_ref):
    count, air_cells = air_ref.shape
    chunks = tile_ref.shape[0]
    one, zero = jnp.ones((), F32), jnp.zeros((), F32)
    rows = [slice(c, c + 1) for c in range(chunks)]
    owns = [
        jnp.broadcast_to(tile_ref[r, :], (tiles, LANES)) == row_ids(tiles) for r in rows
    ]
    owned = jnp.concatenate([jnp.where(o, one, zero) for o in owns], axis=0).astype(jnp.bfloat16)
    earlier = jnp.where(row_ids(LANES) < lane_ids(LANES), one, zero).astype(jnp.bfloat16)
    prior = dot_nn(owned, earlier)
    total = dot_nn(owned, jnp.ones((LANES, LANES), jnp.bfloat16))
    air_parts = jnp.concatenate(
        [p.astype(F32) for p in thirds(air_ref[...])], axis=0
    ).astype(jnp.bfloat16)
    carry = jnp.zeros((tiles, LANES), F32)
    slots, parts = [], []
    for c in range(chunks):
        span = slice(c * tiles, (c + 1) * tiles)
        slots.append(
            jnp.sum(jnp.where(owns[c], prior[span] + carry, zero), axis=0, keepdims=True)
        )
        carry = carry + total[span]
        picked = jnp.broadcast_to(source_ref[rows[c], :], (air_cells, LANES)) == row_ids(air_cells)
        taken = dot_nn(air_parts, jnp.where(picked, one, zero).astype(jnp.bfloat16))
        flux = taken[:count] + taken[count : 2 * count] + taken[2 * count : 3 * count]
        payload = weight_ref[rows[c], :] * flux
        record = jnp.concatenate(
            [
                payload,
                cell_ref[rows[c], :].astype(F32),
                jnp.zeros((HALF - count - 1, LANES), F32),
            ],
            axis=0,
        )
        parts.append([p.astype(F32) for p in thirds(record)])
    slot_hot = jnp.concatenate(
        [
            jnp.where(
                jnp.broadcast_to(s.astype(jnp.int32), (LANES, LANES)) == row_ids(LANES), one, zero
            ).astype(jnp.bfloat16)
            for s in slots
        ],
        axis=1,
    )
    spread = jnp.concatenate(
        [
            jnp.concatenate(
                [
                    jnp.where(
                        jnp.broadcast_to(tile_ref[rows[c], :], (HALF, LANES)) == d,
                        parts[c][part],
                        zero,
                    )
                    for part in range(3)
                    for d in range(tiles)
                ],
                axis=0,
            ).astype(jnp.bfloat16)
            for c in range(chunks)
        ],
        axis=1,
    )
    out = sum_parts(dot_nt(spread, slot_hot))
    cells = pltpu.roll(pltpu.roll(out, CAP, 1).reshape(tiles, HALF, LANES), HALF - count, 1)
    out = out.reshape(tiles, HALF, LANES)
    head = lax.broadcasted_iota(jnp.int32, out.shape, 1) == 0
    msg_ref[...] = jnp.where(head, out + cells, out)[:, :count]


def pack_kernel(
    levels,
    tiles,
    tracer_hbm,
    east_hbm,
    north_hbm,
    kappa_hbm,
    depth_hbm,
    air_hbm,
    tile_hbm,
    source_hbm,
    cell_hbm,
    weight_hbm,
    up_ref,
    down_ref,
    mirror_ref,
    msg_ref,
    own_ref,
    tracer_ref,
    east_ref,
    north_ref,
    kappa_ref,
    depth_ref,
    air_ref,
    tile_ref,
    source_ref,
    cell_ref,
    weight_ref,
    sems,
    small_sems,
):
    count, _, cells, _ = tracer_ref.shape
    fields = count + 2
    chunk = chunk_of(levels)
    blocks = levels // chunk
    lane = lane_ids(cells)

    def copies(block):
        span = pl.ds(block * chunk, chunk)
        pairs = [
            (tracer_hbm.at[:, span], tracer_ref.at[:, span]),
            (north_hbm.at[span], north_ref.at[span]),
            (kappa_hbm.at[span], kappa_ref.at[span]),
            (east_hbm.at[span, pl.ds(cells - HALF, HALF)], east_ref.at[span]),
        ]
        return [
            pltpu.make_async_copy(src, dst, sems.at[block, i]) for i, (src, dst) in enumerate(pairs)
        ]

    small = [
        pltpu.make_async_copy(src, dst, small_sems.at[i])
        for i, (src, dst) in enumerate(
            (
                (tile_hbm, tile_ref),
                (air_hbm, air_ref),
                (source_hbm, source_ref),
                (cell_hbm, cell_ref),
                (weight_hbm, weight_ref),
                (depth_hbm, depth_ref),
            )
        )
    ]
    for copy in small:
        copy.start()
    for block in range(PACK_AHEAD):
        for copy in copies(block):
            copy.start()
    for copy in small:
        copy.wait()
    for block in range(PACK_AHEAD, blocks):
        for copy in copies(block):
            copy.start()

    depth = depth_ref[...].astype(F32)
    up_ref[fields * levels : fields * levels + 1, :] = depth[cells - 1 : cells]
    down_ref[(fields - 1) * levels : (fields - 1) * levels + 1, :] = depth[0:1]
    def several(group, columns):
        columns = list(columns)
        for inner in range(chunk):
            k = group * chunk + inner
            slabs = [tracer_ref[n, k] for n in range(count)] + [north_ref[k], kappa_ref[k]]
            for f in range(fields):
                columns[f] = jnp.where(lane == k, pltpu.roll(slabs[f], k + 1, 1), columns[f])
                if f < count:
                    up_ref[pl.ds(f * levels + k, 1), :] = slabs[f][cells - 1 : cells]
                    down_ref[pl.ds(f * levels + k, 1), :] = slabs[f][0:1]
            up_ref[pl.ds(count * levels + k, 1), :] = east_ref[k, HALF - 1 : HALF, :]
            up_ref[pl.ds((count + 1) * levels + k, 1), :] = slabs[count + 1][cells - 1 : cells]
            down_ref[pl.ds(count * levels + k, 1), :] = slabs[count + 1][0:1]
        return tuple(columns)

    columns = [jnp.zeros((cells, LANES), F32)] * fields
    for block in range(blocks):
        for copy in copies(block):
            copy.wait()
        if block == 0:
            make_messages(tiles, air_ref, tile_ref, source_ref, cell_ref, weight_ref, msg_ref)
        columns = several(block, columns)
    last = depth.shape[1] - 1
    columns = [*columns, jnp.broadcast_to(depth[:, last : last + 1], (cells, LANES))]
    for f in range(fields + 1):
        own_ref[f * cells : (f + 1) * cells, :] = columns[f]
        for i in range(cells):
            spot = f * cells + cells - 1 - i
            mirror_ref[spot : spot + 1, :] = columns[f][i : i + 1]


def pack(tiles, fields, small):
    count, levels, cells, lat = fields[0].shape
    rows = lambda n: jax.ShapeDtypeStruct((-(-n // HALF) * HALF, lat), F32)
    return pl.pallas_call(
        functools.partial(pack_kernel, levels, tiles),
        out_shape=[
            rows((count + 2) * levels + 1),
            rows((count + 1) * levels + 1),
            jax.ShapeDtypeStruct(((count + 3) * cells, LANES), F32),
            jax.ShapeDtypeStruct((tiles, count, LANES), F32),
            pltpu.HBM(((count + 3) * cells, LANES), F32),
        ],
        in_specs=[ANY] * (len(fields) + len(small)),
        out_specs=[VMEM] * 5,
        scratch_shapes=[
            pltpu.VMEM((count, levels, cells, lat), F32),
            pltpu.VMEM((levels, HALF, lat), F32),
            pltpu.VMEM((levels, cells, lat), F32),
            pltpu.VMEM((levels, cells, lat), F32),
        ]
        + [pltpu.VMEM(x.shape, x.dtype) for x in small]
        + [
            pltpu.SemaphoreType.DMA((levels // chunk_of(levels), 4)),
            pltpu.SemaphoreType.DMA((6,)),
        ],
        compiler_params=pltpu.CompilerParams(vmem_limit_bytes=12 << 20),
        cost_estimate=pl.CostEstimate(flops=10**7, bytes_accessed=4 * 10**6, transcendentals=0),
        name="pack",
    )(*in_hbm(*fields, *small))


def gather_surface(count, cells, lat, received_ref):
    tiles = received_ref.shape[0]
    shift = lat.bit_length() - 1
    one, zero = jnp.ones((), F32), jnp.zeros((), F32)
    left, right = [[], [], []], []
    early = lane_ids(count) < CAP
    for t in range(0, tiles, 2):
        even, odd = received_ref[t], received_ref[t + 1]
        block = jnp.where(early, even, pltpu.roll(odd, CAP, 1))
        cell = jnp.where(early, pltpu.roll(even, CAP, 1), odd)[0:1].astype(jnp.int32)
        row = jnp.broadcast_to(lax.shift_right_logical(cell, shift), (cells, LANES))
        col = jnp.broadcast_to(cell & (lat - 1), (lat, LANES))
        right.append(jnp.where(col == row_ids(lat), one, zero).astype(jnp.bfloat16))
        hit = row == row_ids(cells)
        for p, part in enumerate(thirds(block)):
            part = part.astype(F32)
            left[p].append(
                jnp.concatenate(
                    [
                        jnp.where(hit, jnp.broadcast_to(part[n : n + 1], (cells, LANES)), zero)
                        for n in range(count)
                    ],
                    axis=0,
                ).astype(jnp.bfloat16)
            )
    spread = jnp.concatenate(right, axis=1)
    parts = jnp.concatenate([jnp.concatenate(part, axis=1) for part in left], axis=0)
    return sum_parts(dot_nt(parts, spread))


def eliminate_kernel(
    levels,
    west_ref,
    far_ref,
    own_hbm,
    mirror_hbm,
    depth_hbm,
    tracer_hbm,
    kappa_hbm,
    north_hbm,
    east_hbm,
    thick_hbm,
    mixing_hbm,
    state_ref,
    own_ref,
    mirror_ref,
    depth_ref,
    tracer_ref,
    kappa_ref,
    north_ref,
    east_ref,
    thick_ref,
    mixing_ref,
    fold_ref,
    next_ref,
    part_ref,
    south_ref,
    small_sems,
    sems,
):
    count, _, cells, lat = tracer_ref.shape
    chunk = chunk_of(levels)
    blocks, groups = levels // chunk, chunk // GROUP

    def copies(block):
        span = pl.ds(block * chunk, chunk)
        pairs = [(tracer_hbm.at[:, span], tracer_ref.at[:, span])] + [
            (hbm.at[span], ref.at[span])
            for hbm, ref in (
                (kappa_hbm, kappa_ref),
                (north_hbm, north_ref),
                (east_hbm, east_ref),
                (thick_hbm, thick_ref),
                (mixing_hbm, mixing_ref),
            )
        ]
        return [
            pltpu.make_async_copy(src, dst, sems.at[block, i]) for i, (src, dst) in enumerate(pairs)
        ]

    def fetched(block):
        for copy in copies(block):
            copy.wait()

        @pl.when(block >= sum(AHEAD))
        def _():
            for copy in copies(block - sum(AHEAD)):
                copy.start()

    def begin(stage):
        done = sum(AHEAD[:stage])
        for block in range(done, done + AHEAD[stage]):
            for copy in copies(blocks - 1 - block):
                copy.start()

    small = [
        pltpu.make_async_copy(src, dst, small_sems.at[i])
        for i, (src, dst) in enumerate(
            ((own_hbm, own_ref), (mirror_hbm, mirror_ref), (depth_hbm, depth_ref))
        )
    ]
    for copy in small:
        copy.start()
    begin(0)
    halves = cells // HALF
    fields = count + 2
    row8 = row_ids(HALF)
    lane8 = lane_ids(HALF)
    top = lane8 == lat - 1
    first = row8 == 0
    last = row8 == HALF - 1
    hs = [slice(h * HALF, (h + 1) * HALF) for h in range(halves)]

    def from_east(parts, halo):
        turned = [pltpu.roll(p, HALF - 1, 0) for p in parts]
        return [
            jnp.where(last, turned[h + 1] if h + 1 < halves else halo, turned[h])
            for h in range(halves)
        ]

    def from_west(parts, halo):
        turned = [pltpu.roll(p, 1, 0) for p in parts]
        return [
            jnp.where(first, turned[h - 1] if h > 0 else halo, turned[h]) for h in range(halves)
        ]

    def row_of(ref, index):
        return jnp.broadcast_to(ref[pl.ds(index, 1), :], (HALF, lat))

    for copy in small:
        copy.wait()
    begin(1)
    for h in range(halves):
        mine, other = [
            [ref[f * cells + h * HALF : f * cells + (h + 1) * HALF, :] for f in range(fields + 1)]
            for ref in (own_ref, mirror_ref)
        ]
        mean = 0.5 * (mine[count + 1] + other[count + 1])
        speed = 0.5 * (mine[count] - other[count])
        open_face = jnp.minimum(mine[fields], other[fields]) > lane8.astype(F32)
        near = jnp.where(open_face, jnp.maximum(speed, 0.0) + mean, 0.0)
        far = jnp.where(open_face, jnp.minimum(speed, 0.0) - mean, 0.0)
        for n in range(count):
            flux = near * mine[n] + far * other[n]
            for k in range(levels):
                fold_ref[k, n, hs[h], :] = pltpu.roll(flux, lat - 1 - k, 1)
    begin(2)
    depth = [depth_ref[s, :].astype(F32) for s in hs]
    depth_east = from_east(depth, row_of(far_ref, (fields - 1) * levels))
    limit_here = depth
    limit_east = [jnp.minimum(depth[h], depth_east[h]) for h in range(halves)]
    limit_north = [
        jnp.where(top, 0.0, jnp.minimum(depth[h], pltpu.roll(depth[h], lat - 1, 1)))
        for h in range(halves)
    ]
    limit_west = jnp.minimum(
        jnp.broadcast_to(depth[0][0:1], (HALF, lat)), row_of(west_ref, fields * levels)
    )

    def turned(group):
        for inner in range(GROUP):
            k = (levels - GROUP - group * GROUP) + (GROUP - 1 - inner)
            for s in hs:
                next_ref[inner, count, s, :] = pltpu.roll(kappa_ref[k, s, :], lat - 1, 1)
                for n in range(count):
                    next_ref[inner, n, s, :] = pltpu.roll(tracer_ref[n, k, s, :], lat - 1, 1)

    def fluxes(group):
        for inner in range(GROUP):
            k = (levels - GROUP - group * GROUP) + (GROUP - 1 - inner)
            level = k.astype(F32)
            kappa = [kappa_ref[k, s, :] for s in hs]
            speed = [east_ref[k, s, :] for s in hs]
            kappa_east = from_east(kappa, row_of(far_ref, count * levels + k))
            near_e, far_e = [], []
            for h in range(halves):
                mean = 0.5 * (kappa[h] + kappa_east[h])
                open_face = limit_east[h] > level
                near = jnp.maximum(speed[h], 0.0) + mean
                near_e.append(jnp.where(open_face, near, 0.0))
                far_e.append(jnp.where(open_face, speed[h] - near, 0.0))
            speed_w = row_of(west_ref, count * levels + k)
            kappa_w = row_of(west_ref, (count + 1) * levels + k)
            mean = 0.5 * (kappa_w + jnp.broadcast_to(kappa[0][0:1], (HALF, lat)))
            open_face = limit_west > level
            near = jnp.maximum(speed_w, 0.0) + mean
            near_w = jnp.where(open_face, near, 0.0)
            far_w = jnp.where(open_face, speed_w - near, 0.0)
            near_n, far_n = [], []
            for h in range(halves):
                speed_n = north_ref[k, hs[h], :]
                mean = 0.5 * (kappa[h] + next_ref[inner, count, hs[h], :])
                open_face = limit_north[h] > level
                near = jnp.maximum(speed_n, 0.0) + mean
                near_n.append(jnp.where(open_face, near, 0.0))
                far_n.append(jnp.where(open_face, speed_n - near, 0.0))
            for n in range(count):
                cell = [tracer_ref[n, k, s, :] for s in hs]
                cell_east = from_east(cell, row_of(far_ref, n * levels + k))
                flux_e = [near_e[h] * cell[h] + far_e[h] * cell_east[h] for h in range(halves)]
                flux_in = near_w * row_of(west_ref, n * levels + k) + far_w * jnp.broadcast_to(
                    cell[0][0:1], (HALF, lat)
                )
                flux_w = from_west(flux_e, flux_in)
                for h in range(halves):
                    flux_n = near_n[h] * cell[h] + far_n[h] * next_ref[inner, n, hs[h], :]
                    south_ref[inner, n, hs[h], :] = pltpu.roll(flux_n, 1, 1)
                    flux_n = jnp.where(top, fold_ref[k, n, hs[h], :], flux_n)
                    part_ref[inner, n, hs[h], :] = (cell[h] - (flux_e[h] - flux_w[h])) - flux_n

    def solve(group, state):
        thick, coupling, value, gain, scale = jax.tree.map(lambda x: x, state)
        for inner in range(GROUP):
            k = (levels - GROUP - group * GROUP) + (GROUP - 1 - inner)
            above = jnp.maximum(k - 1, 0)
            closed = jnp.where(k > 0, k.astype(F32), float(levels))
            for h in range(halves):
                thick_above = thick_ref[above, hs[h], :]
                here = 2.0 * mixing_ref[above, hs[h], :] / (thick_above + thick[h])
                here = jnp.where(limit_here[h] > closed, here, 0.0)
                scale[h] = 1.0 / (thick[h] + here + coupling[h] - coupling[h] * gain[h])
                gain[h] = here * scale[h]
                state_ref[count * levels + k, hs[h], :] = gain[h]
                share, below = thick[h] * scale[h], coupling[h] * scale[h]
                for n in range(count):
                    stepped = part_ref[inner, n, hs[h], :] + south_ref[inner, n, hs[h], :]
                    value[n][h] = share * stepped + below * value[n][h]
                    state_ref[n * levels + k, hs[h], :] = value[n][h]
                thick[h], coupling[h] = thick_above, here
        return thick, coupling, value, gain, scale

    def turn(group, state):
        ahead = group + 1

        @pl.when(lax.rem(ahead, groups) == 0)
        def _():
            fetched(blocks - 1 - lax.div(ahead, groups))

        state = solve(group - 1, state)
        fluxes(group)
        turned(ahead)
        return state

    zero = [jnp.zeros((HALF, lat), F32)] * halves
    total = blocks * groups
    fetched(jnp.int32(blocks - 1))
    turned(jnp.int32(0))
    fluxes(jnp.int32(0))
    turned(jnp.int32(1))
    state = ([thick_ref[levels - 1, s, :] for s in hs], zero, [zero] * count, zero, zero)
    state = lax.fori_loop(1, total - 1, turn, state)
    state = solve(jnp.int32(total - 2), state)
    fluxes(jnp.int32(total - 1))
    scale = solve(jnp.int32(total - 1), state)[4]
    for h in range(halves):
        state_ref[count * levels, hs[h], :] = jnp.where(limit_here[h] > 0.0, scale[h], 0.0)


def substitute_kernel(state_ref, received_ref, out_hbm, out_ref, sems):
    count, levels, cells, lat = out_ref.shape
    chunk = chunk_of(levels)
    blocks = levels // chunk
    hs = [slice(h, h + HALF) for h in range(0, cells, HALF)]

    def result(block):
        span = pl.ds(block * chunk, chunk)
        return pltpu.make_async_copy(out_ref.at[:, span], out_hbm.at[:, span], sems.at[block])

    surface = gather_surface(count, cells, lat, received_ref)
    solved = [[surface[n * cells + s.start : n * cells + s.stop] for s in hs] for n in range(count)]

    def descend(group, solved):
        solved = jax.tree.map(lambda x: x, solved)
        for inner in range(GROUP):
            k = group * GROUP + inner
            for h, s in enumerate(hs):
                gain = state_ref[count * levels + k, s, :]
                for n in range(count):
                    solved[n][h] = state_ref[n * levels + k, s, :] + gain * solved[n][h]
                    out_ref[n, k, s, :] = solved[n][h]
        return solved

    def substitute(block, solved):
        first = block * (chunk // GROUP)
        solved = lax.fori_loop(first, first + chunk // GROUP, descend, solved)
        result(block).start()
        return solved

    lax.fori_loop(0, blocks, substitute, solved)
    for block in range(blocks):
        result(block).wait()


def eliminate(halos, small, fields):
    count, levels, cells, lat = fields[0].shape
    return pl.pallas_call(
        functools.partial(eliminate_kernel, levels),
        out_shape=pltpu.VMEM(((count + 1) * levels, cells, lat), F32),
        in_specs=[VMEM] * len(halos) + [ANY] * (len(small) + len(fields)),
        out_specs=VMEM,
        scratch_shapes=[pltpu.VMEM(x.shape, x.dtype) for x in (*small, *fields)]
        + [
            pltpu.VMEM((levels, count, cells, lat), F32),
            pltpu.VMEM((GROUP, count + 1, cells, lat), F32),
            pltpu.VMEM((GROUP, count, cells, lat), F32),
            pltpu.VMEM((GROUP, count, cells, lat), F32),
            pltpu.SemaphoreType.DMA((len(small),)),
            pltpu.SemaphoreType.DMA((levels // chunk_of(levels), len(fields))),
        ],
        compiler_params=pltpu.CompilerParams(vmem_limit_bytes=16 << 20),
        cost_estimate=pl.CostEstimate(flops=10**8, bytes_accessed=8 * 10**6, transcendentals=0),
        name="eliminate",
    )(*in_vmem(*halos), *in_hbm(*small, *fields))


def substitute(count, levels, state, received):
    shape = (count, levels, *state.shape[1:])
    return pl.pallas_call(
        substitute_kernel,
        out_shape=jax.ShapeDtypeStruct(shape, F32),
        in_specs=[VMEM] * 2,
        out_specs=ANY,
        scratch_shapes=[
            pltpu.VMEM(shape, F32),
            pltpu.SemaphoreType.DMA((levels // chunk_of(levels),)),
        ],
        compiler_params=pltpu.CompilerParams(vmem_limit_bytes=12 << 20),
        cost_estimate=pl.CostEstimate(flops=10**7, bytes_accessed=6 * 10**6, transcendentals=0),
        name="substitute",
    )(*in_vmem(state, received))


def shards(
    tracer,
    east_speed,
    north_speed,
    diffusivity,
    mixing,
    thickness,
    depth_levels,
    air_flux,
    margin_tile,
    margin_source,
    margin_cell,
    margin_weight,
):
    tiles = lax.axis_size("lon")
    by_level = lambda x: jnp.transpose(x, (1, 0, 2))
    rows = lambda x: x.reshape(-1, LANES)
    tracer = jnp.transpose(tracer, (0, 2, 1, 3))
    east, north, kappa, mixing, thick = [
        by_level(x) for x in (east_speed, north_speed, diffusivity, mixing, thickness)
    ]
    count, levels = tracer.shape[:2]
    small = [depth_levels, air_flux]
    small += [rows(x) for x in (margin_tile, margin_source, margin_cell, margin_weight)]
    up, down, mirror, messages, own = pack(tiles, [tracer, east, north, kappa], small)
    ring = [(i, (i + 1) % tiles) for i in range(tiles)]
    mirror = lax.ppermute(mirror, "lon", [(i, tiles - 1 - i) for i in range(tiles)])
    west = lax.ppermute(up, "lon", ring)
    far = lax.ppermute(down, "lon", [(j, i) for i, j in ring])
    received = lax.all_to_all(messages, "lon", split_axis=0, concat_axis=0, tiled=True)
    fields = [tracer, kappa, north, east, thick, mixing]
    state = eliminate([west, far], [own, mirror, depth_levels], fields)
    out = substitute(count, levels, state, received)
    return jnp.transpose(out, (0, 2, 1, 3))


def solution(mesh):
    placed = (
        P(None, "lon", None, "ens"),
        P("lon", None, "ens"),
        P("lon", None, "ens"),
        P("lon", None, "ens"),
        P("lon", None, "ens"),
        P("lon", None, "ens"),
        P("lon", "ens"),
        P("ens", "lon"),
        P(("ens", "lon"), None),
        P(("ens", "lon")),
        P(("ens", "lon")),
        P(("ens", "lon")),
    )
    return jax.shard_map(
        shards, mesh=mesh, in_specs=placed, out_specs=P(None, "lon", None, "ens"), check_vma=False
    )
```

profile of v0, /device:TPU:0, one launch (start us, length us, event | category | flops | bytes accessed | tf_op | source)
XLA Modules:
  0.0 24.6 jit_solution(8735190491622058853)
XLA Ops:
  0.0 4.0 %pack.1 = (f32[456,128]{1,0:T(8,128)S(1)}, f32[376,128]{1,0:T(8,128)S(1)}, f32[112,128]{1,0:T(8,128)S(1)}, f32[16,4,128]{2,1,0:T(4,128)}, f32[112,128]{1,0:T(8,128)}) custom-call(f32[4,75,16,128]{3,2,1,0:T(8,128)} %bitcast.11, f32[75,16,128]{2,1,0:T(8,128)} %bitcast.13, f32[75,16,128]{2,1,0:T(8,128)} %bitcast.15, f32[75,16,128]{2,1,0:T(8,128)} %bitcast.17, ...), custom_call_target="tpu_custom_call" | custom-call | flops 10000000 | bytes 4000000 | tf_op jit(solution)/shard_map/pack/pallas_call | solution.py:244
  4.0 0.5 %collective-permute-start = (f32[456,128]{1,0:T(8,128)S(1)}, f32[456,128]{1,0:T(8,128)S(1)}, u32[]{:S(2)}, u32[]{:S(2)}) collective-permute-start(f32[456,128]{1,0:T(8,128)S(1)} %get-tuple-element.10), channel_id=1, source_target_pairs={{0,1},{1,2},{2,3},{3,4},{4,5},{5,6},{6,7},{7,8},{8,9},{9,10},{10,1... | collective-permute-start | bytes 700424 | tf_op jit(solution)/shard_map/ppermute | solution.py:631
  4.5 5.1 %collective-permute-start.1 = (f32[376,128]{1,0:T(8,128)S(1)}, f32[376,128]{1,0:T(8,128)S(1)}, u32[]{:S(2)}, u32[]{:S(2)}) collective-permute-start(f32[376,128]{1,0:T(8,128)S(1)} %get-tuple-element.11), channel_id=1, source_target_pairs={{1,0},{2,1},{3,2},{4,3},{5,4},{6,5},{7,6},{8,7},{9,8},{10,9},{11,1... | collective-permute-start | bytes 577544 | tf_op jit(solution)/shard_map/ppermute | solution.py:632
  9.6 0.7 %collective-permute-start.2 = (f32[112,128]{1,0:T(8,128)S(1)}, f32[112,128]{1,0:T(8,128)S(1)}, u32[]{:S(2)}, u32[]{:S(2)}) collective-permute-start(f32[112,128]{1,0:T(8,128)S(1)} %get-tuple-element.13), channel_id=1, source_target_pairs={{0,15},{1,14},{2,13},{3,12},{4,11},{5,10},{6,9},{7,8},{8,7},{9,6},... | collective-permute-start | bytes 172040 | tf_op jit(solution)/shard_map/ppermute | solution.py:630
  10.3 5.1 %all-to-all-start = ((f32[16,4,128]{2,1,0:T(4,128)}), f32[16,4,128]{2,1,0:T(4,128)S(1)}, u32[]{:S(2)}, u32[]{:S(2)}) async-start(f32[16,4,128]{2,1,0:T(4,128)} %get-tuple-element.14), calls=%async_computation | async-start | bytes 65536 | tf_op jit(solution)/shard_map/all_to_all | solution.py:633
  15.4 0.6 %collective-permute-done.2.mirror_hbm = f32[112,128]{1,0:T(8,128)S(1)} collective-permute-done((f32[112,128]{1,0:T(8,128)S(1)}, f32[112,128]{1,0:T(8,128)S(1)}, u32[]{:S(2)}, u32[]{:S(2)}) %collective-permute-start.2) | collective-permute-done | bytes 57376 | tf_op jit(solution)/shard_map/ppermute | solution.py:630
  16.0 0.0 copy-start
  16.0 0.0 collective-permute-done.1.far_ref
  16.0 0.0 collective-permute-done.west_ref
  16.0 0.6 %copy-done = f32[112,128]{1,0:T(8,128)} copy-done((f32[112,128]{1,0:T(8,128)}, f32[112,128]{1,0:T(8,128)S(1)}, u32[]{:S(2)}) %copy-start) | copy-done | bytes 57368
  16.6 6.0 %eliminate.1.state_ref = f32[375,16,128]{2,1,0:T(8,128)S(1)} custom-call(f32[456,128]{1,0:T(8,128)S(1)} %collective-permute-done.west_ref, f32[376,128]{1,0:T(8,128)S(1)} %collective-permute-done.1.far_ref, f32[112,128]{1,0:T(8,128)} %get-tuple-element.12.own_hbm, f32[112,128]{1,0:T(8,128)} %copy-done, s32[16,128]{1,0:T(8,128)} %depth_hbm.3, ...), custom_call_target="tpu_custom_call" | custom-call | flops 100000000 | bytes 8000000 | tf_op jit(solution)/shard_map/eliminate/pallas_call | solution.py:567
  22.7 0.0 all-to-all-done.received_ref
  22.7 1.9 %substitute.1 = f32[4,75,16,128]{3,2,1,0:T(8,128)} custom-call(f32[375,16,128]{2,1,0:T(8,128)S(1)} %eliminate.1.state_ref, f32[16,4,128]{2,1,0:T(4,128)S(1)} %all-to-all-done.received_ref), custom_call_target="tpu_custom_call" | custom-call | flops 10000000 | bytes 6000000 | tf_op jit(solution)/shard_map/substitute/pallas_call | solution.py:589
Async XLA Ops:
  4.0 12.0 %collective-permute-start = (f32[456,128]{1,0:T(8,128)S(1)}, f32[456,128]{1,0:T(8,128)S(1)}, u32[]{:S(2)}, u32[]{:S(2)}) collective-permute-start(f32[456,128]{1,0:T(8,128)S(1)} %get-tuple-element.10), channel_id=1, source_target_pairs={{0,1},{1,2},{2,3},{3,4},{4,5},{5,6},{6,7},{7,8},{8,9},{9,10},{10,1... | collective-permute-start | bytes 700424 | tf_op jit(solution)/shard_map/ppermute | solution.py:631
  4.5 11.5 %collective-permute-start.1 = (f32[376,128]{1,0:T(8,128)S(1)}, f32[376,128]{1,0:T(8,128)S(1)}, u32[]{:S(2)}, u32[]{:S(2)}) collective-permute-start(f32[376,128]{1,0:T(8,128)S(1)} %get-tuple-element.11), channel_id=1, source_target_pairs={{1,0},{2,1},{3,2},{4,3},{5,4},{6,5},{7,6},{8,7},{9,8},{10,9},{11,1... | collective-permute-start | bytes 577544 | tf_op jit(solution)/shard_map/ppermute | solution.py:632
  9.6 6.4 %collective-permute-start.2 = (f32[112,128]{1,0:T(8,128)S(1)}, f32[112,128]{1,0:T(8,128)S(1)}, u32[]{:S(2)}, u32[]{:S(2)}) collective-permute-start(f32[112,128]{1,0:T(8,128)S(1)} %get-tuple-element.13), channel_id=1, source_target_pairs={{0,15},{1,14},{2,13},{3,12},{4,11},{5,10},{6,9},{7,8},{8,7},{9,6},... | collective-permute-start | bytes 172040 | tf_op jit(solution)/shard_map/ppermute | solution.py:630
  10.3 12.4 %all-to-all-start = ((f32[16,4,128]{2,1,0:T(4,128)}), f32[16,4,128]{2,1,0:T(4,128)S(1)}, u32[]{:S(2)}, u32[]{:S(2)}) async-start(f32[16,4,128]{2,1,0:T(4,128)} %get-tuple-element.14), calls=%async_computation | async-start | bytes 65536 | tf_op jit(solution)/shard_map/all_to_all | solution.py:633
  16.0 0.6 %copy-start = (f32[112,128]{1,0:T(8,128)}, f32[112,128]{1,0:T(8,128)S(1)}, u32[]{:S(2)}) copy-start(f32[112,128]{1,0:T(8,128)S(1)} %collective-permute-done.2.mirror_hbm) | copy-start | bytes 172036
where the time goes:
time: 24.8 us; the launch traced here: 24.6 us
  Pallas kernels  12 us (48%)
  starting transfers between devices  11.4 us (46%)
  local copies, waits for them, and re-layouts  0.6 us (2%)
  waiting for transfers between devices  0.58 us (2%)
    pallas_call x1, Pallas kernels, eliminate(): pl.pallas_call(functools.partial(eliminate_kernel, levels), out_shape=plt...  6.04 us
    all_to_all x1, starting transfers between devices, shards(): lax.all_to_all(messages, 'lon', split_axis=0, concat_axis=0, tiled=True)  5.15 us
    ppermute x1, starting transfers between devices, shards(): far = lax.ppermute(down, 'lon', [(j, i) for i, j in ring])  5.06 us
    pallas_call x1, Pallas kernels, pack(): pl.pallas_call(functools.partial(pack_kernel, levels, tiles), out_shape=[...  4.03 us
    pallas_call x1, Pallas kernels, substitute(): pl.pallas_call(substitute_kernel, out_shape=jax.ShapeDtypeStruct(shape, F...  1.89 us
    ppermute x1, starting transfers between devices, shards(): lax.ppermute(mirror, 'lon', [(i, tiles - 1 - i) for i in range(tiles)])  0.68 us
    unnamed x2, local copies, waits for them, and re-layouts  0.6 us
    ppermute x1, waiting for transfers between devices, shards(): lax.ppermute(mirror, 'lon', [(i, tiles - 1 - i) for i in range(tiles)])  0.57 us
  transfers between devices with their start and end apart: 4, of which 1 were waited for; matrix products, arithmetic and copies ran while one was open for 0% of the time, Pallas kernels for 25%

commit v1 on v0

--- a/solution.py
+++ b/solution.py
@@ -12,6 +12,7 @@
 GROUP = 5
 AHEAD = (2, 1, 0)
 PACK_AHEAD = 2
+SETTLE = 17 * 10**8
 LANES = 128
 F32 = jnp.float32
 
@@ -584,6 +585,24 @@
     )(*in_vmem(*halos), *in_hbm(*small, *fields))
 
 
+def settle_kernel(block_ref, out_hbm, sem):
+    copy = pltpu.make_async_copy(block_ref, out_hbm, sem)
+    copy.start()
+    copy.wait()
+
+
+def settle(block):
+    return pl.pallas_call(
+        settle_kernel,
+        out_shape=pltpu.HBM(block.shape, block.dtype),
+        in_specs=[VMEM],
+        out_specs=ANY,
+        scratch_shapes=[pltpu.SemaphoreType.DMA],
+        cost_estimate=pl.CostEstimate(flops=SETTLE, bytes_accessed=10**5, transcendentals=0),
+        name="settle",
+    )(*in_vmem(block))
+
+
 def substitute(count, levels, state, received):
     shape = (count, levels, *state.shape[1:])
     return pl.pallas_call(
@@ -631,6 +650,7 @@
     west = lax.ppermute(up, "lon", ring)
     far = lax.ppermute(down, "lon", [(j, i) for i, j in ring])
     received = lax.all_to_all(messages, "lon", split_axis=0, concat_axis=0, tiled=True)
+    mirror = settle(mirror)
     fields = [tracer, kappa, north, east, thick, mixing]
     state = eliminate([west, far], [own, mirror, depth_levels], fields)
     out = substitute(count, levels, state, received)

time: 24.8 us -> 24.4 us (0.984)
  the two profiles are of different devices: /device:TPU:0 before, /device:TPU:1 now
where the time goes in v1:
time: 24.4 us; the launch traced here: 24.2 us
  Pallas kernels  12.6 us (52%)
  starting transfers between devices  9.28 us (38%)
  waiting for transfers between devices  2.27 us (9%)
    pallas_call x1, Pallas kernels, eliminate(): pl.pallas_call(functools.partial(eliminate_kernel, levels), out_shape=plt...  6.04 us
    pallas_call x1, Pallas kernels, pack(): pl.pallas_call(functools.partial(pack_kernel, levels, tiles), out_shape=[...  4.03 us
    all_to_all x1, starting transfers between devices, shards(): lax.all_to_all(messages, 'lon', split_axis=0, concat_axis=0, tiled=True)  3.48 us
    ppermute x1, starting transfers between devices, shards(): lax.ppermute(mirror, 'lon', [(i, tiles - 1 - i) for i in range(tiles)])  3.12 us
    ppermute x1, starting transfers between devices, shards(): west = lax.ppermute(up, 'lon', ring)  2.68 us
    pallas_call x1, Pallas kernels, substitute(): pl.pallas_call(substitute_kernel, out_shape=jax.ShapeDtypeStruct(shape, F...  1.89 us
    ppermute x1, waiting for transfers between devices, shards(): far = lax.ppermute(down, 'lon', [(j, i) for i, j in ring])  1.55 us
    ppermute x1, waiting for transfers between devices, shards(): lax.ppermute(mirror, 'lon', [(i, tiles - 1 - i) for i in range(tiles)])  0.72 us
  transfers between devices with their start and end apart: 4, of which 2 were waited for; matrix products, arithmetic and copies ran while one was open for 0% of the time, Pallas kernels for 28%

profile of v1, /device:TPU:1, one launch (start us, length us, event | category | flops | bytes accessed | tf_op | source)
XLA Modules:
  0.0 24.2 jit_solution(17760963417986053175)
XLA Ops:
  0.0 4.0 %pack.1 = (f32[456,128]{1,0:T(8,128)S(1)}, f32[376,128]{1,0:T(8,128)S(1)}, f32[112,128]{1,0:T(8,128)S(1)}, f32[16,4,128]{2,1,0:T(4,128)}, f32[112,128]{1,0:T(8,128)}) custom-call(f32[4,75,16,128]{3,2,1,0:T(8,128)} %bitcast.11, f32[75,16,128]{2,1,0:T(8,128)} %bitcast.13, f32[75,16,128]{2,1,0:T(8,128)} %bitcast.15, f32[75,16,128]{2,1,0:T(8,128)} %bitcast.17, ...), custom_call_target="tpu_custom_call" | custom-call | flops 10000000 | bytes 4000000 | tf_op jit(solution)/shard_map/pack/pallas_call | solution.py:245
  4.0 2.7 %collective-permute-start = (f32[456,128]{1,0:T(8,128)S(1)}, f32[456,128]{1,0:T(8,128)S(1)}, u32[]{:S(2)}, u32[]{:S(2)}) collective-permute-start(f32[456,128]{1,0:T(8,128)S(1)} %get-tuple-element.10), channel_id=1, source_target_pairs={{0,1},{1,2},{2,3},{3,4},{4,5},{5,6},{6,7},{7,8},{8,9},{9,10},{10,1... | collective-permute-start | bytes 700424 | tf_op jit(solution)/shard_map/ppermute | solution.py:650
  6.7 3.1 %collective-permute-start.2 = (f32[112,128]{1,0:T(8,128)S(1)}, f32[112,128]{1,0:T(8,128)S(1)}, u32[]{:S(2)}, u32[]{:S(2)}) collective-permute-start(f32[112,128]{1,0:T(8,128)S(1)} %get-tuple-element.13), channel_id=1, source_target_pairs={{0,15},{1,14},{2,13},{3,12},{4,11},{5,10},{6,9},{7,8},{8,7},{9,6},... | collective-permute-start | bytes 172040 | tf_op jit(solution)/shard_map/ppermute | solution.py:649
  9.8 0.0 collective-permute-start.1
  9.8 3.5 %all-to-all-start = ((f32[16,4,128]{2,1,0:T(4,128)}), f32[16,4,128]{2,1,0:T(4,128)S(1)}, u32[]{:S(2)}, u32[]{:S(2)}) async-start(f32[16,4,128]{2,1,0:T(4,128)} %get-tuple-element.14), calls=%async_computation | async-start | bytes 65536 | tf_op jit(solution)/shard_map/all_to_all | solution.py:652
  13.3 0.7 %collective-permute-done.2.block_ref = f32[112,128]{1,0:T(8,128)S(1)} collective-permute-done((f32[112,128]{1,0:T(8,128)S(1)}, f32[112,128]{1,0:T(8,128)S(1)}, u32[]{:S(2)}, u32[]{:S(2)}) %collective-permute-start.2) | collective-permute-done | bytes 57376 | tf_op jit(solution)/shard_map/ppermute | solution.py:649
  14.0 0.6 %settle.1.mirror_hbm = f32[112,128]{1,0:T(8,128)} custom-call(f32[112,128]{1,0:T(8,128)S(1)} %collective-permute-done.2.block_ref), custom_call_target="tpu_custom_call" | custom-call | flops 1700000000 | bytes 100000 | tf_op jit(solution)/shard_map/settle/pallas_call | solution.py:595
  14.7 1.6 %collective-permute-done.1.far_ref = f32[376,128]{1,0:T(8,128)S(1)} collective-permute-done((f32[376,128]{1,0:T(8,128)S(1)}, f32[376,128]{1,0:T(8,128)S(1)}, u32[]{:S(2)}, u32[]{:S(2)}) %collective-permute-start.1) | collective-permute-done | bytes 192544 | tf_op jit(solution)/shard_map/ppermute | solution.py:651
  16.2 0.0 collective-permute-done.west_ref
  16.2 6.0 %eliminate.1.state_ref = f32[375,16,128]{2,1,0:T(8,128)S(1)} custom-call(f32[456,128]{1,0:T(8,128)S(1)} %collective-permute-done.west_ref, f32[376,128]{1,0:T(8,128)S(1)} %collective-permute-done.1.far_ref, f32[112,128]{1,0:T(8,128)} %get-tuple-element.12.own_hbm, f32[112,128]{1,0:T(8,128)} %settle.1.mirror_hbm, s32[16,128]{1,0:T(8,128)} %depth_hbm.3, ...), custom_call_target="tpu_custom_call" | custom-call | flops 100000000 | bytes 8000000 | tf_op jit(solution)/shard_map/eliminate/pallas_call | solution.py:568
  22.3 0.0 all-to-all-done.received_ref
  22.3 1.9 %substitute.1 = f32[4,75,16,128]{3,2,1,0:T(8,128)} custom-call(f32[375,16,128]{2,1,0:T(8,128)S(1)} %eliminate.1.state_ref, f32[16,4,128]{2,1,0:T(4,128)S(1)} %all-to-all-done.received_ref), custom_call_target="tpu_custom_call" | custom-call | flops 10000000 | bytes 6000000 | tf_op jit(solution)/shard_map/substitute/pallas_call | solution.py:608
Async XLA Ops:
  4.0 12.2 %collective-permute-start = (f32[456,128]{1,0:T(8,128)S(1)}, f32[456,128]{1,0:T(8,128)S(1)}, u32[]{:S(2)}, u32[]{:S(2)}) collective-permute-start(f32[456,128]{1,0:T(8,128)S(1)} %get-tuple-element.10), channel_id=1, source_target_pairs={{0,1},{1,2},{2,3},{3,4},{4,5},{5,6},{6,7},{7,8},{8,9},{9,10},{10,1... | collective-permute-start | bytes 700424 | tf_op jit(solution)/shard_map/ppermute | solution.py:650
  6.7 7.3 %collective-permute-start.2 = (f32[112,128]{1,0:T(8,128)S(1)}, f32[112,128]{1,0:T(8,128)S(1)}, u32[]{:S(2)}, u32[]{:S(2)}) collective-permute-start(f32[112,128]{1,0:T(8,128)S(1)} %get-tuple-element.13), channel_id=1, source_target_pairs={{0,15},{1,14},{2,13},{3,12},{4,11},{5,10},{6,9},{7,8},{8,7},{9,6},... | collective-permute-start | bytes 172040 | tf_op jit(solution)/shard_map/ppermute | solution.py:649
  9.8 6.4 %collective-permute-start.1 = (f32[376,128]{1,0:T(8,128)S(1)}, f32[376,128]{1,0:T(8,128)S(1)}, u32[]{:S(2)}, u32[]{:S(2)}) collective-permute-start(f32[376,128]{1,0:T(8,128)S(1)} %get-tuple-element.11), channel_id=1, source_target_pairs={{1,0},{2,1},{3,2},{4,3},{5,4},{6,5},{7,6},{8,7},{9,8},{10,9},{11,1... | collective-permute-start | bytes 577544 | tf_op jit(solution)/shard_map/ppermute | solution.py:651
  9.8 12.4 %all-to-all-start = ((f32[16,4,128]{2,1,0:T(4,128)}), f32[16,4,128]{2,1,0:T(4,128)S(1)}, u32[]{:S(2)}, u32[]{:S(2)}) async-start(f32[16,4,128]{2,1,0:T(4,128)} %get-tuple-element.14), calls=%async_computation | async-start | bytes 65536 | tf_op jit(solution)/shard_map/all_to_all | solution.py:652
